TPU v7x, 32 devices: a whole 2x2x4 slice. The times are simulated.
32 devices in a mesh: axial: 8 (over y, x, core), trans: 4 (over z).
Axes of the slice: x: 2, y: 2, z: 4, core: 2. Of those that a mesh axis runs over, the one named last changes fastest.
Arguments:
- concentration: float32 [128, 32, 256], P('axial', 'trans'), may hold values from -4 to 4
- pore_mask: int32 [128, 32, 256], P('axial', 'trans'), may hold values 0 or 1
- velocity: float32 [128, 32, 256], P('axial', 'trans'), may hold values from 20 to 80
Outputs:
- new_concentration: float32 [128, 32, 256], P('axial', 'trans')
All inputs are finite; a program needn't handle non-finite values. No bound on the sum of `pore_mask` on one device may be relied on, other than what follows from the above.
Results may differ from a plain program's by a relative error of at most 0.00028.
Values sent between devices are 32-bit elements; how exact they have to be, the bound alone decides.
A program may use at most 64 MiB of HBM per device.

v0:
```python
import jax
import jax.numpy as jnp
from jax import lax
from jax.sharding import PartitionSpec as P

axial_number = 800.0
trans_number = 0.5


def padded(cells, sides, width):
    for axis, dim in sides:
        count = lax.axis_size(axis)
        ends = count - 1
        head = lax.slice_in_dim(cells, 0, width, axis=dim)
        tail = lax.slice_in_dim(cells, cells.shape[dim] - width, cells.shape[dim], axis=dim)
        cells = jnp.concatenate(
            [
                lax.ppermute(tail, axis, [(i, (i + 1) % count) for i in range(ends)]),
                cells,
                lax.ppermute(head, axis, [((i + 1) % count, i) for i in range(ends)]),
            ],
            axis=dim,
        )
    return cells


def plane_term(field_pad, phi_pad, field_data, axis_dim):
    cells = field_data.shape[axis_dim]
    face_share = 0.5 * (
        lax.slice_in_dim(phi_pad, 0, cells + 1, axis=axis_dim)
        + lax.slice_in_dim(phi_pad, 1, cells + 2, axis=axis_dim)
    )
    upper_part = lax.slice_in_dim(face_share, 1, cells + 1, axis=axis_dim) * (
        lax.slice_in_dim(field_pad, 2, cells + 2, axis=axis_dim) - field_data
    )
    lower_part = lax.slice_in_dim(face_share, 0, cells, axis=axis_dim) * (
        lax.slice_in_dim(field_pad, 0, cells, axis=axis_dim) - field_data
    )
    return upper_part + lower_part


def eliminate(below_coef, main_coef, above_coef, rhs):
    cell_count = main_coef.shape[0]
    first_src = jnp.concatenate([-below_coef[1:2], jnp.zeros_like(main_coef[2 : cell_count - 1])])
    last_src = jnp.concatenate(
        [
            jnp.zeros_like(main_coef[1 : cell_count - 2]),
            -above_coef[cell_count - 2 : cell_count - 1],
        ]
    )
    sources = jnp.stack([first_src, last_src, rhs[1 : cell_count - 1]], axis=1)

    def forward(running, row_data):
        ratios, partials = running
        below_row, main_row, above_row, source_row = row_data
        pivot_value = main_row - below_row * ratios
        new_ratios = above_row / pivot_value
        new_partials = (source_row - below_row[None] * partials) / pivot_value[None]
        return ((new_ratios, new_partials), (new_ratios, new_partials))

    start_state = (jnp.zeros_like(main_coef[0]), jnp.zeros_like(sources[0]))
    inputs_inner = (
        below_coef[1 : cell_count - 1],
        main_coef[1 : cell_count - 1],
        above_coef[1 : cell_count - 1],
        sources,
    )
    _, (ratio_rows, partial_rows) = lax.scan(forward, start_state, inputs_inner)

    def backward(next_value, row_data):
        ratios, partials = row_data
        now_value = partials - ratios[None] * next_value
        return (now_value, now_value)

    _, interior = lax.scan(
        backward, jnp.zeros_like(partial_rows[0]), (ratio_rows, partial_rows), reverse=True
    )
    last_cell = cell_count - 1
    first_lower = below_coef[0]
    first_main = main_coef[0] + above_coef[0] * interior[0, 0]
    first_upper = above_coef[0] * interior[0, 1]
    first_rhs = rhs[0] - above_coef[0] * interior[0, 2]
    last_lower = below_coef[last_cell] * interior[-1, 0]
    last_main = main_coef[last_cell] + below_coef[last_cell] * interior[-1, 1]
    last_upper = above_coef[last_cell]
    last_rhs = rhs[last_cell] - below_coef[last_cell] * interior[-1, 2]
    reduced = jnp.stack(
        [
            jnp.stack([first_lower, last_lower]),
            jnp.stack([first_main, last_main]),
            jnp.stack([first_upper, last_upper]),
            jnp.stack([first_rhs, last_rhs]),
        ]
    )
    return (reduced, interior)


def assemble(first_cell, last_cell, interior):
    inner_cells = (
        interior[:, 0] * first_cell[None] + interior[:, 1] * last_cell[None] + interior[:, 2]
    )
    return jnp.concatenate([first_cell[None], inner_cells, last_cell[None]])


def reduce_cyclic(lower_part, main_part, upper_part, right_part):
    row_count = lower_part.shape[0]
    for stride_level in range(row_count.bit_length() - 1):
        stride = 2**stride_level

        def from_lower(values, fill_value):
            return jnp.concatenate(
                [jnp.full_like(values[:stride], fill_value), values[: row_count - stride]]
            )

        def from_upper(values, fill_value):
            return jnp.concatenate([values[stride:], jnp.full_like(values[:stride], fill_value)])

        factor_low = lower_part / from_lower(main_part, 1.0)
        factor_high = upper_part / from_upper(main_part, 1.0)
        new_lower = -factor_low * from_lower(lower_part, 0.0)
        new_main = (
            main_part
            - factor_low * from_lower(upper_part, 0.0)
            - factor_high * from_upper(lower_part, 0.0)
        )
        new_upper = -factor_high * from_upper(upper_part, 0.0)
        new_right = (
            right_part
            - factor_low * from_lower(right_part, 0.0)
            - factor_high * from_upper(right_part, 0.0)
        )
        lower_part, main_part, upper_part, right_part = (new_lower, new_main, new_upper, new_right)
    return right_part / main_part


def body(concentration, pore_mask, velocity):
    porosity = 0.1 + 0.9 * pore_mask.astype(jnp.float32)
    axial_ext = padded(jnp.stack([concentration, porosity, velocity]), (("axial", 1),), 1)
    conc_ext = axial_ext[0]
    phi_ext = axial_ext[1]
    vel_ext = axial_ext[2]
    face_share = 0.5 * (phi_ext[:-1] + phi_ext[1:])
    advect = 0.5 * (vel_ext[:-1] + vel_ext[1:]) * face_share
    spread = axial_number * face_share
    lower_coef = advect[:-1] + spread[:-1]
    upper_coef = spread[1:]
    center = spread[:-1] + spread[1:] + advect[1:]
    axial_term = lower_coef * conc_ext[:-2] - center * concentration + upper_coef * conc_ext[2:]
    plane_ext = padded(jnp.stack([concentration, porosity]), (("trans", 2),), 1)
    transverse = plane_term(plane_ext[0], plane_ext[1], concentration, 1)
    z_widths = ((0, 0), (0, 0), (1, 1))
    transverse = transverse + plane_term(
        jnp.pad(concentration, z_widths), jnp.pad(porosity, z_widths), concentration, 2
    )
    rhs = concentration + axial_term + trans_number * transverse
    below_coef = -lower_coef
    main_coef = 1.0 + center
    above_coef = -upper_coef
    device_index = lax.axis_index("axial")
    reduced, interior = eliminate(below_coef, main_coef, above_coef, rhs)
    gathered = lax.all_gather(reduced, "axial", axis=1, tiled=True)
    all_ends = reduce_cyclic(gathered[0], gathered[1], gathered[2], gathered[3])
    end_values = lax.dynamic_slice_in_dim(all_ends, 2 * device_index, 2, 0)
    return assemble(end_values[0], end_values[1], interior)


def solution(mesh):
    in_specs = (P("axial", "trans", None), P("axial", "trans", None), P("axial", "trans", None))
    out_specs = P("axial", "trans", None)
    return jax.shard_map(body, mesh=mesh, in_specs=in_specs, out_specs=out_specs, check_vma=False)
```

profile of v0, /device:TPU:0, one launch (start us, length us, event | category | flops | bytes accessed | tf_op | source)
XLA Modules:
  0.0 33.0 jit_solution(11848905922522627214)
XLA Ops:
  0.0 0.0 copy-start
  0.0 0.0 copy-start.1
  0.0 1.0 %fusion.47 = (f32[1,16,8,256]{3,2,1,0:T(8,128)S(1)}, f32[16,8,256]{2,1,0:T(8,128)S(1)}) fusion(s32[16,8,256]{2,1,0:T(8,128)} %param.8), kind=kLoop, calls=%fused_computation.145 | loop fusion | flops 98304 | bytes 393216 | tf_op jit(solution)/shard_map/stack | solution.py:138
  1.0 0.0 copy-done
  1.0 0.0 copy-done.1
  1.0 2.3 %collective-permute-start = (f32[3,1,8,256]{3,2,1,0:T(8,128)S(1)}, f32[3,1,8,256]{3,2,1,0:T(8,128)S(1)}, u32[]{:S(2)}, u32[]{:S(2)}) collective-permute-start(f32[3,1,8,256]{3,2,1,0:T(8,128)S(1)} %get-tuple-element.278), channel_id=1, source_target_pairs={{0,4},{4,8},{8,12},{12,16},{16,20},{20,24},{24,28},{1,5},{5,9},{9,... | collective-permute-start | bytes 73736 | tf_op jit(solution)/shard_map/ppermute | solution.py:18
  3.4 1.3 %collective-permute-start.1 = (f32[3,1,8,256]{3,2,1,0:T(8,128)S(1)}, f32[3,1,8,256]{3,2,1,0:T(8,128)S(1)}, u32[]{:S(2)}, u32[]{:S(2)}) collective-permute-start(f32[3,1,8,256]{3,2,1,0:T(8,128)S(1)} %get-tuple-element.279), channel_id=1, source_target_pairs={{4,0},{8,4},{12,8},{16,12},{20,16},{24,20},{28,24},{5,1},{9,5},{13... | collective-permute-start | bytes 73736 | tf_op jit(solution)/shard_map/ppermute | solution.py:20
  4.7 4.3 %collective-permute-start.2 = (f32[2,16,1,256]{3,2,1,0:T(1,128)S(1)}, f32[2,16,1,256]{3,2,1,0:T(1,128)S(1)}, u32[]{:S(2)}, u32[]{:S(2)}) collective-permute-start(f32[2,16,1,256]{3,2,1,0:T(1,128)S(1)} %get-tuple-element.282), channel_id=1, source_target_pairs={{0,1},{1,2},{2,3},{4,5},{5,6},{6,7},{8,9},{9,10},{10,11},{12,13},{... | collective-permute-start | bytes 98312 | tf_op jit(solution)/shard_map/ppermute | solution.py:18
  9.1 1.3 %collective-permute-start.3 = (f32[2,16,1,256]{3,2,1,0:T(1,128)S(1)}, f32[2,16,1,256]{3,2,1,0:T(1,128)S(1)}, u32[]{:S(2)}, u32[]{:S(2)}) collective-permute-start(f32[2,16,1,256]{3,2,1,0:T(1,128)S(1)} %get-tuple-element.283), channel_id=1, source_target_pairs={{1,0},{2,1},{3,2},{5,4},{6,5},{7,6},{9,8},{10,9},{11,10},{13,12},{... | collective-permute-start | bytes 98312 | tf_op jit(solution)/shard_map/ppermute | solution.py:20
  10.4 0.1 fusion.3
  10.5 0.0 collective-permute-done
  10.5 0.0 collective-permute-done.1
  10.5 0.1 maximum_maximum_fusion
  10.8 0.0 copy-start.2
  10.8 0.6 %copy-done.2 = f32[16,8,256]{2,1,0:T(8,128)} copy-done((f32[16,8,256]{2,1,0:T(8,128)}, f32[16,8,256]{2,1,0:T(8,128)S(1)}, u32[]{:S(2)}) %copy-start.2) | copy-done | bytes 131096
  11.4 0.0 collective-permute-done.2
  11.4 3.4 %collective-permute-done.3 = f32[2,16,1,256]{3,2,1,0:T(1,128)S(1)} collective-permute-done((f32[2,16,1,256]{3,2,1,0:T(1,128)S(1)}, f32[2,16,1,256]{3,2,1,0:T(1,128)S(1)}, u32[]{:S(2)}, u32[]{:S(2)}) %collective-permute-start.3) | collective-permute-done | bytes 32800 | tf_op jit(solution)/shard_map/ppermute | solution.py:20
  14.9 0.1 pad_maximum_fusion
  15.1 0.2 fusion.11
  15.3 0.0 slice-start
  15.4 0.9 %slice-done = f32[14,8,256]{2,1,0:T(8,128)S(1)} async-done(((f32[16,8,256]{2,1,0:T(8,128)}), f32[14,8,256]{2,1,0:T(8,128)S(1)}, s32[]{:S(2)}) %slice-start) | async-done | bytes 114712 | tf_op jit(solution)/shard_map/slice | solution.py:64
  16.2 0.9 %while.34 = (s32[]{:T(128)}, f32[8,256]{1,0:T(8,128)S(1)}, f32[3,8,256]{2,1,0:T(8,128)S(1)}, f32[14,8,256]{2,1,0:T(8,128)S(1)}, f32[14,3,8,256]{3,2,1,0:T(8,128)...) while((s32[]{:T(128)}, f32[8,256]{1,0:T(8,128)S(1)}, ...), condition=%wide.region_1.2_spmd.clone, body=%wide.region_0.1_spmd.clone.sunk | while | flops 32771 | bytes 180352 | solution.py:68
  17.1 0.0 copy-start.3
  17.1 0.8 %while.35 = (s32[]{:T(128)}, f32[3,8,256]{2,1,0:T(8,128)S(1)}, f32[14,3,8,256]{3,2,1,0:T(8,128)S(1)}, f32[14,3,8,256]{3,2,1,0:T(8,128)S(1)}, f32[14,8,256]{2,1,0...) while((s32[]{:T(128)}, f32[3,8,256]{2,1,0:T(8,128)S(1)}, f32[14,3,8,256]{3,2,1,0:T(8,128)S(1)}, ...), condition=%wide.region_3.4_spmd.clone, body=%wide.region_2.3_spmd.clone.sunk | while | flops 18436 | bytes 122995 | solution.py:75
  18.0 0.1 copy-done.3
  18.1 13.3 %all_gather.3 = f32[4,16,8,256]{3,2,1,0:T(8,128)S(1)} all-gather(f32[4,2,8,256]{3,2,1,0:T(8,128)S(1)} %pad_maximum_fusion.4), channel_id=1, replica_groups=mesh['axial'=8,'trans'=4] {'axial'}, dimensions={1}, use_global_device_ids=true | all-gather | bytes 589824 | tf_op jit(solution)/shard_map/all_gather | solution.py:161
  31.4 0.1 slice_bitcast_fusion.9
  31.5 0.1 fusion.15
  31.6 0.1 multiply_subtract_fusion.3
  31.8 0.1 multiply_subtract_fusion.2
  31.9 0.1 multiply_subtract_fusion.1
  32.1 0.1 pad_multiply_fusion.1
  32.3 0.7 %pad_maximum_fusion.3 = f32[16,8,256]{2,1,0:T(8,128)} fusion(f32[1,8,256]{2,1,0:T(8,128)S(1)} %get-tuple-element.316, f32[14,8,256]{2,1,0:T(8,128)S(1)} %fusion.29, f32[1,8,256]{2,1,0:T(8,128)S(1)} %get-tuple-element.313), kind=kLoop, calls=%fused_computation.64 | loop fusion | flops 65536 | bytes 262144 | tf_op jit(solution)/shard_map/concatenate | solution.py:102
  (97 shorter events, 1.4 us)
Async XLA Ops:
  0.0 1.0 %copy-start = (f32[16,8,256]{2,1,0:T(8,128)S(1)}, f32[16,8,256]{2,1,0:T(8,128)}, u32[]{:S(2)}) copy-start(f32[16,8,256]{2,1,0:T(8,128)} %param.7) | copy-start | bytes 393220
  0.0 1.0 %copy-start.1 = (f32[16,8,256]{2,1,0:T(8,128)S(1)}, f32[16,8,256]{2,1,0:T(8,128)}, u32[]{:S(2)}) copy-start(f32[16,8,256]{2,1,0:T(8,128)} %param.9) | copy-start | bytes 393220
  1.0 9.5 %collective-permute-start = (f32[3,1,8,256]{3,2,1,0:T(8,128)S(1)}, f32[3,1,8,256]{3,2,1,0:T(8,128)S(1)}, u32[]{:S(2)}, u32[]{:S(2)}) collective-permute-start(f32[3,1,8,256]{3,2,1,0:T(8,128)S(1)} %get-tuple-element.278), channel_id=1, source_target_pairs={{0,4},{4,8},{8,12},{12,16},{16,20},{20,24},{24,28},{1,5},{5,9},{9,... | collective-permute-start | bytes 73736 | tf_op jit(solution)/shard_map/ppermute | solution.py:18
  3.4 7.1 %collective-permute-start.1 = (f32[3,1,8,256]{3,2,1,0:T(8,128)S(1)}, f32[3,1,8,256]{3,2,1,0:T(8,128)S(1)}, u32[]{:S(2)}, u32[]{:S(2)}) collective-permute-start(f32[3,1,8,256]{3,2,1,0:T(8,128)S(1)} %get-tuple-element.279), channel_id=1, source_target_pairs={{4,0},{8,4},{12,8},{16,12},{20,16},{24,20},{28,24},{5,1},{9,5},{13... | collective-permute-start | bytes 73736 | tf_op jit(solution)/shard_map/ppermute | solution.py:20
  4.7 6.7 %collective-permute-start.2 = (f32[2,16,1,256]{3,2,1,0:T(1,128)S(1)}, f32[2,16,1,256]{3,2,1,0:T(1,128)S(1)}, u32[]{:S(2)}, u32[]{:S(2)}) collective-permute-start(f32[2,16,1,256]{3,2,1,0:T(1,128)S(1)} %get-tuple-element.282), channel_id=1, source_target_pairs={{0,1},{1,2},{2,3},{4,5},{5,6},{6,7},{8,9},{9,10},{10,11},{12,13},{... | collective-permute-start | bytes 98312 | tf_op jit(solution)/shard_map/ppermute | solution.py:18
  9.1 5.8 %collective-permute-start.3 = (f32[2,16,1,256]{3,2,1,0:T(1,128)S(1)}, f32[2,16,1,256]{3,2,1,0:T(1,128)S(1)}, u32[]{:S(2)}, u32[]{:S(2)}) collective-permute-start(f32[2,16,1,256]{3,2,1,0:T(1,128)S(1)} %get-tuple-element.283), channel_id=1, source_target_pairs={{1,0},{2,1},{3,2},{5,4},{6,5},{7,6},{9,8},{10,9},{11,10},{13,12},{... | collective-permute-start | bytes 98312 | tf_op jit(solution)/shard_map/ppermute | solution.py:20
  10.8 0.7 %copy-start.2 = (f32[16,8,256]{2,1,0:T(8,128)}, f32[16,8,256]{2,1,0:T(8,128)S(1)}, u32[]{:S(2)}) copy-start(f32[16,8,256]{2,1,0:T(8,128)S(1)} %broadcast_add_fusion) | copy-start | bytes 393220
  15.3 0.9 %slice-start = ((f32[16,8,256]{2,1,0:T(8,128)}), f32[14,8,256]{2,1,0:T(8,128)S(1)}, s32[]{:S(2)}) async-start(f32[16,8,256]{2,1,0:T(8,128)} %copy-done.2), calls=%async_computation | async-start | bytes 229376 | tf_op jit(solution)/shard_map/slice | solution.py:64
  17.1 0.9 %copy-start.3 = (f32[16,8,256]{2,1,0:T(8,128)S(1)}, f32[16,8,256]{2,1,0:T(8,128)}, u32[]{:S(2)}) copy-start(f32[16,8,256]{2,1,0:T(8,128)} %copy-done.2) | copy-start | bytes 393220
where the time goes:
time: 33.2 us; the launch traced here: 33 us
  blocking collectives  13.3 us (40%)
  starting transfers between devices  9.24 us (28%)
  other arithmetic  3.51 us (11%)
  waiting for transfers between devices  3.45 us (10%)
  local copies, waits for them, and re-layouts  2.09 us (6%)
  loops' own time  0.93 us (3%)
  between operations  0.44 us (1%)
    all_gather x1, blocking collectives, body(): gathered = lax.all_gather(reduced, 'axial', axis=1, tiled=True)  13.3 us
    ppermute x2, starting transfers between devices, padded(): lax.ppermute(tail, axis, [(i, (i + 1) % count) for i in range(ends)])  6.66 us
    ppermute x2, waiting for transfers between devices, padded(): lax.ppermute(head, axis, [((i + 1) % count, i) for i in range(ends)])  3.45 us
    ppermute x2, starting transfers between devices, padded(): lax.ppermute(head, axis, [((i + 1) % count, i) for i in range(ends)])  2.58 us
    another operation x1, other arithmetic, body(): jnp.stack([concentration, porosity, velocity])  0.97 us
    slice x2, local copies, waits for them, and re-layouts, eliminate(): main_coef[1:cell_count - 1]  0.86 us
    unnamed x8, local copies, waits for them, and re-layouts  0.75 us
    concatenate x1, other arithmetic, assemble(): return jnp.concatenate([first_cell[None], inner_cells, last_cell[None]])  0.67 us
  transfers between devices with their start and end apart: 4, of which 1 were waited for; matrix products, arithmetic and copies ran while one was open for 1% of the time, Pallas kernels for 0%

commit v1 on v0

v1 whole, which is shorter than its diff:
```python
import functools

import jax
import jax.numpy as jnp
from jax import lax
from jax.experimental import pallas as pl
from jax.experimental.pallas import tpu as pltpu
from jax.sharding import PartitionSpec as P

axial_number = 800.0
trans_number = 0.5
MESH = pl.DeviceIdType.MESH


def kernel(
    n, nt, c_hbm, m_hbm, v_hbm, out, c_s, m_s, v_s, ts, tr, axs, axr, rhs_s, cond, got, xs, xr,
    load_sem, t_send, t_recv, a_send, a_recv, g_send, g_recv, x_send, x_recv,
):
    cells, rows, width = c_s.shape
    solvers = min(n, rows)
    me = lax.axis_index("axial")
    mt = lax.axis_index("trans")
    last = cells - 1

    loads = [
        pltpu.make_async_copy(src, dst, load_sem.at[k])
        for k, (src, dst) in enumerate(((c_hbm, c_s), (m_hbm, m_s), (v_hbm, v_s)))
    ]
    for copy in loads:
        copy.start()

    barrier = pltpu.get_barrier_semaphore()
    has_before, has_after = mt > 0, mt < nt - 1
    has_prev, has_next = me > 0, me < n - 1

    @pl.when(has_before)
    def _():
        pl.semaphore_signal(barrier, inc=1, device_id=(me, mt - 1), device_id_type=MESH)

    @pl.when(has_after)
    def _():
        pl.semaphore_signal(barrier, inc=1, device_id=(me, mt + 1), device_id_type=MESH)

    for d in range(1, n):
        pl.semaphore_signal(
            barrier, inc=1, device_id=(lax.rem(me + d, n), mt), device_id_type=MESH
        )

    @pl.when(jnp.logical_not(has_before))
    def _():
        tr[0] = jnp.zeros_like(tr[0])

    @pl.when(jnp.logical_not(has_after))
    def _():
        tr[1] = jnp.zeros_like(tr[1])

    @pl.when(jnp.logical_not(has_prev))
    def _():
        axr[0] = jnp.zeros_like(axr[0])

    @pl.when(jnp.logical_not(has_next))
    def _():
        axr[1] = jnp.zeros_like(axr[1])

    for copy in loads:
        copy.wait()

    c = c_s[...]
    ph = 0.1 + 0.9 * m_s[...].astype(jnp.float32)
    v = v_s[...]
    for e, y in ((0, 0), (1, rows - 1)):
        ts[e, 0] = c_s[:, y, :]
        ts[e, 1] = 0.1 + 0.9 * m_s[:, y, :].astype(jnp.float32)
    for e, i in ((0, 0), (1, last)):
        axs[e, 0] = c[i]
        axs[e, 1] = ph[i]
        axs[e, 2] = v[i]

    pl.semaphore_wait(barrier, n - 1 + has_before.astype(jnp.int32) + has_after.astype(jnp.int32))

    def t_copy(e):
        return pltpu.make_async_remote_copy(
            src_ref=ts.at[e], dst_ref=tr.at[1 - e], send_sem=t_send.at[e], recv_sem=t_recv.at[1 - e],
            device_id=(me, mt + (2 * e - 1)), device_id_type=MESH,
        )

    def a_copy(e):
        return pltpu.make_async_remote_copy(
            src_ref=axs.at[e], dst_ref=axr.at[1 - e], send_sem=a_send.at[e],
            recv_sem=a_recv.at[1 - e], device_id=(me + (2 * e - 1), mt), device_id_type=MESH,
        )

    sides = ((0, has_before, has_prev), (1, has_after, has_next))
    for e, has_t, _ in sides:
        pl.when(has_t)(lambda e=e: t_copy(e).start())
    for e, _, has_a in sides:
        pl.when(has_a)(lambda e=e: a_copy(e).start())

    share = 0.5 * (ph[:-1] + ph[1:])
    spr = axial_number * share
    low = 0.5 * (v[:-1] + v[1:]) * share + spr
    flux = low * c[:-1] - spr * c[1:]
    lane = lax.broadcasted_iota(jnp.int32, c.shape, 2)
    ph_l = jnp.where(lane == 0, 0.0, pltpu.roll(ph, 1, 2))
    c_l = jnp.where(lane == 0, 0.0, pltpu.roll(c, 1, 2))
    z_l = 0.5 * (ph_l + ph) * (c_l - c)
    z_r = jnp.where(lane == width - 1, 0.5 * ph * c, pltpu.roll(z_l, width - 1, 2))
    sub = lax.broadcasted_iota(jnp.int32, c.shape, 1)
    y_l = jnp.where(
        sub == 0, 0.0, 0.5 * (pltpu.roll(ph, 1, 1) + ph) * (pltpu.roll(c, 1, 1) - c)
    )
    y_r = pltpu.roll(y_l, rows - 1, 1)
    part = c + trans_number * ((z_l - z_r) + (y_l - y_r))
    rhs_s[0] = part[0] - flux[0]
    rhs_s[1:last] = part[1:last] + (flux[:-1] - flux[1:])
    rhs_s[last] = part[last] + flux[-1]

    lo = lambda i: low[i - 1]
    up = lambda i: spr[i]
    mid = lambda i: 1.0 + spr[i - 1] + low[i]
    pinv, alpha, gamma, spike = {}, {}, {}, {}
    for i in range(1, last):
        pivot = mid(i) if i == 1 else mid(i) - lo(i) * gamma[i - 1]
        pinv[i] = 1.0 / pivot
        alpha[i] = lo(i) * pinv[i]
        gamma[i] = up(i) * pinv[i]
        spike[i] = alpha[i] if i == 1 else alpha[i] * spike[i - 1]
    qinv, beta = {}, {}
    for i in range(last - 1, 0, -1):
        pivot = mid(i) if i == last - 1 else mid(i) - up(i) * eps
        qinv[i] = 1.0 / pivot
        beta[i] = up(i) * qinv[i]
        eps = lo(i) * qinv[i]
        reach = beta[i] if i == last - 1 else beta[i] * reach

    for e, _, has_a in sides:
        pl.when(has_a)(lambda e=e: a_copy(1 - e).wait_recv())

    def face(c0, p0, v0, c1, p1, v1):
        s = 0.5 * (p0 + p1)
        d = axial_number * s
        lw = 0.5 * (v0 + v1) * s + d
        return d, lw, lw * c0 - d * c1

    spr_0, low_0, flux_0 = face(axr[0, 0], axr[0, 1], axr[0, 2], c[0], ph[0], v[0])
    _, low_n, flux_n = face(c[last], ph[last], v[last], axr[1, 0], axr[1, 1], axr[1, 2])
    w = 1.0 / (1.0 + spr_0 + low[0] - up(0) * eps)
    keep = jnp.where(has_prev, 1.0, 0.0)
    a0 = keep * (w * low_0)
    b0 = w * up(0) * reach
    give = keep * spr_0
    far = spike[last - 1]
    cond[:, 0, :] = -lo(last) * far * a0
    cond[:, 1, :] = 1.0 + spr[-1] + low_n - lo(last) * (far * b0 + gamma[last - 1])
    cond[:, 2, :] = -give * a0
    cond[:, 3, :] = -give * b0

    for e, has_t, _ in sides:
        pl.when(has_t)(lambda e=e: t_copy(1 - e).wait_recv())
    for e, y in ((0, 0), (1, rows - 1)):
        term = (0.5 * trans_number) * (tr[e, 1] + ts[e, 1]) * (tr[e, 0] - ts[e, 0])
        rhs_s[:, y, :] = rhs_s[:, y, :] + term
    r = rhs_s[...]
    partial = {}
    for i in range(1, last):
        partial[i] = r[i] * pinv[i]
        if i > 1:
            partial[i] = partial[i] + alpha[i] * partial[i - 1]
    for i in range(last - 1, 0, -1):
        back = r[i] * qinv[i] if i == last - 1 else r[i] * qinv[i] + beta[i] * back
    c0 = w * (r[0] + flux_0 + up(0) * back)
    cond[:, 4, :] = r[last] - flux_n + lo(last) * (far * c0 + partial[last - 1])
    cond[:, 5, :] = give * c0

    def g_copy(to, src, k):
        return pltpu.make_async_remote_copy(
            src_ref=cond.at[to], dst_ref=got.at[src], send_sem=g_send.at[k], recv_sem=g_recv.at[k],
            device_id=(to, mt), device_id_type=MESH,
        )

    def x_copy(to, src, k):
        return pltpu.make_async_remote_copy(
            src_ref=xs.at[to], dst_ref=xr.at[src], send_sem=x_send.at[k], recv_sem=x_recv.at[k],
            device_id=(to, mt), device_id_type=MESH,
        )

    solving = me < solvers
    for d in range(1, n):
        to = lax.rem(me + d, n)
        pl.when(to < solvers)(lambda to=to, d=d: g_copy(to, me, d).start())

    from_first, from_last, fixed = {}, {}, {}
    for i in range(last - 1, 0, -1):
        if i == last - 1:
            from_first[i], from_last[i], fixed[i] = spike[i], gamma[i], partial[i]
        else:
            from_first[i] = spike[i] + gamma[i] * from_first[i + 1]
            from_last[i] = gamma[i] * from_last[i + 1]
            fixed[i] = partial[i] + gamma[i] * fixed[i + 1]

    @pl.when(solving)
    def _():
        got[me] = cond[me]
        for d in range(1, n):
            g_copy(0, 0, d).wait_recv()
        ahead = lambda t, k: pltpu.roll(t, n - k, 0)
        behind = lambda t, k: pltpu.roll(t, k, 0)
        inv = 1.0 / (got[:, 1, :] + ahead(got[:, 2, :], 1))
        lower = got[:, 0, :] * inv
        upper = ahead(got[:, 3, :], 1) * inv
        right = (got[:, 4, :] + ahead(got[:, 5, :], 1)) * inv
        stride = 1
        while stride < n:
            inv = 1.0 / (1.0 - lower * behind(upper, stride) - upper * ahead(lower, stride))
            right = inv * (right - lower * behind(right, stride) - upper * ahead(right, stride))
            if 2 * stride < n:
                lower, upper = (
                    -inv * lower * behind(lower, stride), -inv * upper * ahead(upper, stride)
                )
            stride *= 2
        seg = lax.broadcasted_iota(jnp.int32, right.shape, 0)
        xs[:, 0, :] = jnp.where(seg == 0, 0.0, behind(right, 1))
        xs[:, 1, :] = right
        for d in range(1, n):
            x_copy(lax.rem(me + d, n), me, d).start()
        xr[me] = xs[me]

    for d in range(1, n):
        src = lax.rem(me + n - d, n)
        pl.when(src < solvers)(lambda src=src, d=d: x_copy(0, 0, d).wait_recv())
    x_before, x_last = xr[:, 0, :], xr[:, 1, :]
    x_first = a0 * x_before + b0 * x_last + c0
    out[0] = x_first
    for i in range(1, last):
        out[i] = from_first[i] * x_first + from_last[i] * x_last + fixed[i]
    out[last] = x_last

    for e, has_t, has_a in sides:
        pl.when(has_t)(lambda e=e: t_copy(e).wait_send())
        pl.when(has_a)(lambda e=e: a_copy(e).wait_send())
    for d in range(1, n):
        to = lax.rem(me + d, n)
        pl.when(to < solvers)(lambda d=d: g_copy(0, 0, d).wait_send())

    @pl.when(solving)
    def _():
        for d in range(1, n):
            x_copy(0, 0, d).wait_send()


def body(concentration, pore_mask, velocity):
    n, nt = lax.axis_size("axial"), lax.axis_size("trans")
    cells, rows, width = concentration.shape
    f32 = jnp.float32
    any_spec = pl.BlockSpec(memory_space=pl.ANY)
    dma = pltpu.SemaphoreType.DMA
    return pl.pallas_call(
        functools.partial(kernel, n, nt),
        out_shape=jax.ShapeDtypeStruct(concentration.shape, f32),
        in_specs=[any_spec] * 3,
        out_specs=pl.BlockSpec(memory_space=pltpu.VMEM),
        scratch_shapes=[
            pltpu.VMEM((cells, rows, width), f32),
            pltpu.VMEM((cells, rows, width), jnp.int32),
            pltpu.VMEM((cells, rows, width), f32),
            pltpu.VMEM((2, 2, cells, width), f32),
            pltpu.VMEM((2, 2, cells, width), f32),
            pltpu.VMEM((2, 3, rows, width), f32),
            pltpu.VMEM((2, 3, rows, width), f32),
            pltpu.VMEM((cells, rows, width), f32),
            pltpu.VMEM((rows, 6, width), f32),
            pltpu.VMEM((n, 6, width), f32),
            pltpu.VMEM((n, 2, width), f32),
            pltpu.VMEM((rows, 2, width), f32),
            dma((3,)), dma((2,)), dma((2,)), dma((2,)), dma((2,)),
            dma((n,)), dma((n,)), dma((n,)), dma((n,)),
        ],
        compiler_params=pltpu.CompilerParams(
            collective_id=0, has_side_effects=True, vmem_limit_bytes=32 * 1024 * 1024
        ),
    )(concentration, pore_mask, velocity)


def solution(mesh):
    specs = P("axial", "trans", None)
    return jax.shard_map(
        body, mesh=mesh, in_specs=(specs,) * 3, out_specs=specs, check_vma=False
    )
```

time: 33.2 us -> 18.4 us (0.55)
  Pallas kernels: 0 us -> 14.9 us
  blocking collectives: 13.3 us -> 0 us
  starting transfers between devices: 9.24 us -> 0 us
  other arithmetic: 3.51 us -> 0 us
  waiting for transfers between devices: 3.45 us -> 0 us
  local copies, waits for them, and re-layouts: 2.09 us -> 3.37 us
  loops' own time: 0.93 us -> 0 us
  between operations: 0.44 us -> 0.01 us
    pallas_call x0 -> x1, Pallas kernels: none -> 14.9 us  [body(): pl.pallas_call(functools.partial(kernel, n, nt), out_shape=jax.ShapeDtype...]
    all_gather x1 -> x0, blocking collectives: 13.3 us -> none  [body(): gathered = lax.all_gather(reduced, 'axial', axis=1, tiled=True)]
    ppermute x4 -> x0, starting transfers between devices: 9.24 us -> none  [the longest x2 6.66 us: padded(): lax.ppermute(tail, axis, [(i, (i + 1) % count) for i in range(ends)])]
    ppermute x4 -> x0, waiting for transfers between devices: 3.45 us -> none  [the longest x2 3.45 us: padded(): lax.ppermute(head, axis, [((i + 1) % count, i) for i in range(ends)])]
    unnamed x8 -> x7, local copies, waits for them, and re-layouts: 0.75 us -> 3.37 us
    slice x17 -> x0, local copies, waits for them, and re-layouts: 1.12 us -> none  [the longest x2 0.86 us: eliminate(): main_coef[1:cell_count - 1]]
    another operation x7 -> x0, other arithmetic: 1.02 us -> none  [the longest x1 0.97 us: body(): jnp.stack([concentration, porosity, velocity])]
    another operation x2 -> x0, loops' own time: 0.93 us -> none  [the longest x1 0.49 us: eliminate(): lax.scan(backward, jnp.zeros_like(partial_rows[0]), (ratio_rows, partial_...]
  transfers between devices with their start and end apart: 4 -> 0, of which waited for: 1 -> 0; matrix products, arithmetic and copies ran while one was open for 1% -> 0% of each run, Pallas kernels for 0% -> 0%
where the time goes in v1:
time: 18.4 us; the launch traced here: 18.3 us
  Pallas kernels  14.9 us (81%)
  local copies, waits for them, and re-layouts  3.37 us (18%)
    pallas_call x1, Pallas kernels, body(): pl.pallas_call(functools.partial(kernel, n, nt), out_shape=jax.ShapeDtype...  14.9 us
    unnamed x7, local copies, waits for them, and re-layouts  3.37 us

profile of v1, /device:TPU:0, one launch (start us, length us, event | category | flops | bytes accessed | tf_op | source)
XLA Modules:
  0.0 18.3 jit_solution(2437797119466889281)
XLA Ops:
  0.0 0.0 copy-start
  0.0 0.9 %copy-done = f32[16,8,256]{2,1,0:T(8,128)S(1)} copy-done((f32[16,8,256]{2,1,0:T(8,128)S(1)}, f32[16,8,256]{2,1,0:T(8,128)}, u32[]{:S(2)}) %copy-start) | copy-done | bytes 131096
  0.9 0.0 copy-start.1
  0.9 0.9 %copy-done.1 = s32[16,8,256]{2,1,0:T(8,128)S(1)} copy-done((s32[16,8,256]{2,1,0:T(8,128)S(1)}, s32[16,8,256]{2,1,0:T(8,128)}, u32[]{:S(2)}) %copy-start.1) | copy-done | bytes 131096
  1.8 0.0 copy-start.2
  1.8 0.9 %copy-done.2 = f32[16,8,256]{2,1,0:T(8,128)S(1)} copy-done((f32[16,8,256]{2,1,0:T(8,128)S(1)}, f32[16,8,256]{2,1,0:T(8,128)}, u32[]{:S(2)}) %copy-start.2) | copy-done | bytes 131096
  2.7 14.9 %shard_map.37 = f32[16,8,256]{2,1,0:T(8,128)S(1)} custom-call(f32[16,8,256]{2,1,0:T(8,128)S(1)} %copy-done, s32[16,8,256]{2,1,0:T(8,128)S(1)} %copy-done.1, f32[16,8,256]{2,1,0:T(8,128)S(1)} %copy-done.2), custom_call_target="tpu_custom_call" | custom-call | tf_op jit(solution)/shard_map/pallas_call | solution.py:257
  17.6 0.7 %copy.5 = f32[16,8,256]{2,1,0:T(8,128)} copy(f32[16,8,256]{2,1,0:T(8,128)S(1)} %shard_map.37) | data formatting | bytes 262144
Async XLA Ops:
  0.0 0.9 %copy-start = (f32[16,8,256]{2,1,0:T(8,128)S(1)}, f32[16,8,256]{2,1,0:T(8,128)}, u32[]{:S(2)}) copy-start(f32[16,8,256]{2,1,0:T(8,128)} %c_hbm.1) | copy-start | bytes 393220
  0.9 0.9 %copy-start.1 = (s32[16,8,256]{2,1,0:T(8,128)S(1)}, s32[16,8,256]{2,1,0:T(8,128)}, u32[]{:S(2)}) copy-start(s32[16,8,256]{2,1,0:T(8,128)} %m_hbm.1) | copy-start | bytes 393220
  1.8 0.9 %copy-start.2 = (f32[16,8,256]{2,1,0:T(8,128)S(1)}, f32[16,8,256]{2,1,0:T(8,128)}, u32[]{:S(2)}) copy-start(f32[16,8,256]{2,1,0:T(8,128)} %v_hbm.1) | copy-start | bytes 393220

commit v2 on v1

--- a/solution.py
+++ b/solution.py
@@ -13,14 +13,19 @@
 
 
 def kernel(
-    n, nt, c_hbm, m_hbm, v_hbm, out, c_s, m_s, v_s, ts, tr, axs, axr, rhs_s, cond, got, xs, xr,
-    load_sem, t_send, t_recv, a_send, a_recv, g_send, g_recv, x_send, x_recv,
+    n, nt, c_hbm, m_hbm, v_hbm, out, c_s, m_s, v_s, ts, tr, axs, axr, rhs_s, cond, pair, chip, xx, xs, xr,
+    load_sem, t_send, t_recv, a_send, a_recv, p_send, p_recv, g_send, g_recv, x_send, x_recv,
 ):
     cells, rows, width = c_s.shape
-    solvers = min(n, rows)
+    half = width // 2
+    chips = n // 2
     me = lax.axis_index("axial")
     mt = lax.axis_index("trans")
     last = cells - 1
+    q, core = me // 2, lax.rem(me, 2)
+    sibling = me + 1 - 2 * core
+    beyond = me - 1 + 2 * core
+    has_beyond = jnp.logical_and(beyond >= 0, beyond < n)
 
     loads = [
         pltpu.make_async_copy(src, dst, load_sem.at[k])
@@ -41,10 +46,16 @@
     def _():
         pl.semaphore_signal(barrier, inc=1, device_id=(me, mt + 1), device_id_type=MESH)
 
-    for d in range(1, n):
+    for d in range(chips - 1, 0, -1):
         pl.semaphore_signal(
-            barrier, inc=1, device_id=(lax.rem(me + d, n), mt), device_id_type=MESH
+            barrier, inc=1, device_id=(2 * lax.bitwise_xor(q, d) + core, mt), device_id_type=MESH
         )
+
+    @pl.when(has_beyond)
+    def _():
+        pl.semaphore_signal(barrier, inc=1, device_id=(beyond, mt), device_id_type=MESH)
+
+    pl.semaphore_signal(barrier, inc=1, device_id=(sibling, mt), device_id_type=MESH)
 
     @pl.when(jnp.logical_not(has_before))
     def _():
@@ -76,7 +87,8 @@
         axs[e, 1] = ph[i]
         axs[e, 2] = v[i]
 
-    pl.semaphore_wait(barrier, n - 1 + has_before.astype(jnp.int32) + has_after.astype(jnp.int32))
+    here = [flag.astype(jnp.int32) for flag in (has_before, has_after, has_beyond)]
+    pl.semaphore_wait(barrier, chips + sum(here))
 
     def t_copy(e):
         return pltpu.make_async_remote_copy(
@@ -150,10 +162,15 @@
     b0 = w * up(0) * reach
     give = keep * spr_0
     far = spike[last - 1]
-    cond[:, 0, :] = -lo(last) * far * a0
-    cond[:, 1, :] = 1.0 + spr[-1] + low_n - lo(last) * (far * b0 + gamma[last - 1])
-    cond[:, 2, :] = -give * a0
-    cond[:, 3, :] = -give * b0
+
+    def put(k, value):
+        cond[0, k] = value[:, :half]
+        cond[1, k] = value[:, half:]
+
+    put(0, -lo(last) * far * a0)
+    put(1, 1.0 + spr[-1] + low_n - lo(last) * (far * b0 + gamma[last - 1]))
+    put(2, -give * a0)
+    put(3, -give * b0)
 
     for e, has_t, _ in sides:
         pl.when(has_t)(lambda e=e: t_copy(1 - e).wait_recv())
@@ -169,25 +186,36 @@
     for i in range(last - 1, 0, -1):
         back = r[i] * qinv[i] if i == last - 1 else r[i] * qinv[i] + beta[i] * back
     c0 = w * (r[0] + flux_0 + up(0) * back)
-    cond[:, 4, :] = r[last] - flux_n + lo(last) * (far * c0 + partial[last - 1])
-    cond[:, 5, :] = give * c0
-
-    def g_copy(to, src, k):
+    put(4, r[last] - flux_n + lo(last) * (far * c0 + partial[last - 1]))
+    put(5, give * c0)
+
+    p_copy = pltpu.make_async_remote_copy(
+        src_ref=cond.at[1 - core], dst_ref=pair, send_sem=p_send.at[0], recv_sem=p_recv.at[0],
+        device_id=(sibling, mt), device_id_type=MESH,
+    )
+    p_copy.start()
+
+    def g_copy(d):
         return pltpu.make_async_remote_copy(
-            src_ref=cond.at[to], dst_ref=got.at[src], send_sem=g_send.at[k], recv_sem=g_recv.at[k],
-            device_id=(to, mt), device_id_type=MESH,
+            src_ref=chip.at[q], dst_ref=chip.at[q], send_sem=g_send.at[d], recv_sem=g_recv.at[d],
+            device_id=(2 * lax.bitwise_xor(q, d) + core, mt), device_id_type=MESH,
         )
 
-    def x_copy(to, src, k):
-        return pltpu.make_async_remote_copy(
-            src_ref=xs.at[to], dst_ref=xr.at[src], send_sem=x_send.at[k], recv_sem=x_recv.at[k],
-            device_id=(to, mt), device_id_type=MESH,
-        )
-
-    solving = me < solvers
-    for d in range(1, n):
-        to = lax.rem(me + d, n)
-        pl.when(to < solvers)(lambda to=to, d=d: g_copy(to, me, d).start())
+    own = cond[core]
+    first = core == 0
+    p_copy.wait_recv()
+    other = pair[...]
+    l_a, d_a, u1_a, u2_a, f_a, u3_a = [jnp.where(first, own[k], other[k]) for k in range(6)]
+    l_b, d_b, u1_b, u2_b, f_b, u3_b = [jnp.where(first, other[k], own[k]) for k in range(6)]
+    inv = 1.0 / (d_a + u1_b)
+    la, ua, fa = inv * l_a, inv * u2_b, inv * (f_a + u3_b)
+    merged = (
+        -l_b * la, d_b - l_b * ua, u1_a - u2_a * la, -u2_a * ua, f_b - l_b * fa, u3_a - u2_a * fa
+    )
+    for k, value in enumerate(merged):
+        chip[q, k] = value
+    for d in range(chips - 1, 0, -1):
+        g_copy(d).start()
 
     from_first, from_last, fixed = {}, {}, {}
     for i in range(last - 1, 0, -1):
@@ -198,37 +226,56 @@
             from_last[i] = gamma[i] * from_last[i + 1]
             fixed[i] = partial[i] + gamma[i] * fixed[i + 1]
 
-    @pl.when(solving)
-    def _():
-        got[me] = cond[me]
-        for d in range(1, n):
-            g_copy(0, 0, d).wait_recv()
-        ahead = lambda t, k: pltpu.roll(t, n - k, 0)
-        behind = lambda t, k: pltpu.roll(t, k, 0)
-        inv = 1.0 / (got[:, 1, :] + ahead(got[:, 2, :], 1))
-        lower = got[:, 0, :] * inv
-        upper = ahead(got[:, 3, :], 1) * inv
-        right = (got[:, 4, :] + ahead(got[:, 5, :], 1)) * inv
-        stride = 1
-        while stride < n:
-            inv = 1.0 / (1.0 - lower * behind(upper, stride) - upper * ahead(lower, stride))
-            right = inv * (right - lower * behind(right, stride) - upper * ahead(right, stride))
-            if 2 * stride < n:
-                lower, upper = (
-                    -inv * lower * behind(lower, stride), -inv * upper * ahead(upper, stride)
-                )
-            stride *= 2
-        seg = lax.broadcasted_iota(jnp.int32, right.shape, 0)
-        xs[:, 0, :] = jnp.where(seg == 0, 0.0, behind(right, 1))
-        xs[:, 1, :] = right
-        for d in range(1, n):
-            x_copy(lax.rem(me + d, n), me, d).start()
-        xr[me] = xs[me]
-
-    for d in range(1, n):
-        src = lax.rem(me + n - d, n)
-        pl.when(src < solvers)(lambda src=src, d=d: x_copy(0, 0, d).wait_recv())
-    x_before, x_last = xr[:, 0, :], xr[:, 1, :]
+    for d in range(1, chips):
+        g_copy(d).wait_recv()
+    side, free = {}, {}
+
+    def row(j):
+        above = j + 1 < chips
+        diag = chip[j, 1] + chip[j + 1, 2] if above else chip[j, 1]
+        right = chip[j, 4] + chip[j + 1, 5] if above else chip[j, 4]
+        return chip[j, 0], diag, chip[j + 1, 3] if above else None, right
+
+    middle = chips // 2
+    for j in range(middle):
+        lower, diag, upper, right = row(j)
+        if j > 0:
+            diag, right = diag - lower * side[j - 1], right - lower * free[j - 1]
+        inv = 1.0 / diag
+        side[j], free[j] = inv * upper, inv * right
+    for j in range(chips - 1, middle - 1, -1):
+        lower, diag, upper, right = row(j)
+        if j + 1 < chips:
+            diag, right = diag - upper * side[j + 1], right - upper * free[j + 1]
+        inv = 1.0 / diag
+        side[j], free[j] = inv * lower, inv * right
+    x = (free[middle] - side[middle] * free[middle - 1]) / (1.0 - side[middle] * side[middle - 1])
+    xx[0] = jnp.zeros_like(x)
+    xx[middle + 1] = x
+    down = up_x = x
+    for j in range(middle - 1, -1, -1):
+        down = free[j] - side[j] * down
+        xx[j + 1] = down
+    for j in range(middle + 1, chips):
+        up_x = free[j] - side[j] * up_x
+        xx[j + 1] = up_x
+    x_p, x_b = xx[q], xx[q + 1]
+    x_a = fa - la * x_p - ua * x_b
+    xs[0] = jnp.where(first, x_a, x_p)
+    xs[1] = jnp.where(first, x_b, x_a)
+    x_copy = pltpu.make_async_remote_copy(
+        src_ref=xs, dst_ref=xr.at[core], send_sem=x_send.at[0], recv_sem=x_recv.at[0],
+        device_id=(sibling, mt), device_id_type=MESH,
+    )
+    x_copy.start()
+    xr[core, 0] = jnp.where(first, x_p, x_a)
+    xr[core, 1] = jnp.where(first, x_a, x_b)
+    pltpu.make_async_remote_copy(
+        src_ref=xs, dst_ref=xr.at[1 - core], send_sem=x_send.at[0], recv_sem=x_recv.at[0],
+        device_id=(sibling, mt), device_id_type=MESH,
+    ).wait_recv()
+    x_before = jnp.concatenate([xr[0, 0], xr[1, 0]], axis=1)
+    x_last = jnp.concatenate([xr[0, 1], xr[1, 1]], axis=1)
     x_first = a0 * x_before + b0 * x_last + c0
     out[0] = x_first
     for i in range(1, last):
@@ -238,26 +285,22 @@
     for e, has_t, has_a in sides:
         pl.when(has_t)(lambda e=e: t_copy(e).wait_send())
         pl.when(has_a)(lambda e=e: a_copy(e).wait_send())
-    for d in range(1, n):
-        to = lax.rem(me + d, n)
-        pl.when(to < solvers)(lambda d=d: g_copy(0, 0, d).wait_send())
-
-    @pl.when(solving)
-    def _():
-        for d in range(1, n):
-            x_copy(0, 0, d).wait_send()
+    p_copy.wait_send()
+    for d in range(1, chips):
+        g_copy(d).wait_send()
+    x_copy.wait_send()
 
 
 def body(concentration, pore_mask, velocity):
     n, nt = lax.axis_size("axial"), lax.axis_size("trans")
     cells, rows, width = concentration.shape
     f32 = jnp.float32
-    any_spec = pl.BlockSpec(memory_space=pl.ANY)
+    hbm_spec = pl.BlockSpec(memory_space=pl.ANY)
     dma = pltpu.SemaphoreType.DMA
     return pl.pallas_call(
         functools.partial(kernel, n, nt),
         out_shape=jax.ShapeDtypeStruct(concentration.shape, f32),
-        in_specs=[any_spec] * 3,
+        in_specs=[hbm_spec] * 3,
         out_specs=pl.BlockSpec(memory_space=pltpu.VMEM),
         scratch_shapes=[
             pltpu.VMEM((cells, rows, width), f32),
@@ -268,15 +311,17 @@
             pltpu.VMEM((2, 3, rows, width), f32),
             pltpu.VMEM((2, 3, rows, width), f32),
             pltpu.VMEM((cells, rows, width), f32),
-            pltpu.VMEM((rows, 6, width), f32),
-            pltpu.VMEM((n, 6, width), f32),
-            pltpu.VMEM((n, 2, width), f32),
-            pltpu.VMEM((rows, 2, width), f32),
+            pltpu.VMEM((2, 6, rows, width // 2), f32),
+            pltpu.VMEM((6, rows, width // 2), f32),
+            pltpu.VMEM((n // 2, 6, rows, width // 2), f32),
+            pltpu.VMEM((n // 2 + 1, rows, width // 2), f32),
+            pltpu.VMEM((2, rows, width // 2), f32),
+            pltpu.VMEM((2, 2, rows, width // 2), f32),
             dma((3,)), dma((2,)), dma((2,)), dma((2,)), dma((2,)),
-            dma((n,)), dma((n,)), dma((n,)), dma((n,)),
+            dma((1,)), dma((1,)), dma((n // 2,)), dma((n // 2,)), dma((1,)), dma((1,)),
         ],
         compiler_params=pltpu.CompilerParams(
-            collective_id=0, has_side_effects=True, vmem_limit_bytes=32 * 1024 * 1024
+            collective_id=0, has_side_effects=True
         ),
     )(concentration, pore_mask, velocity)
 

time: 18.4 us -> 14.6 us (0.79)
  Pallas kernels: 14.9 us -> 12.9 us
  local copies, waits for them, and re-layouts: 3.37 us -> 1.57 us
    pallas_call x1, Pallas kernels: 14.9 us -> 12.9 us  [body(): pl.pallas_call(functools.partial(kernel, n, nt), out_shape=jax.ShapeDtype...]
    unnamed x7 -> x1, local copies, waits for them, and re-layouts: 3.37 us -> 1.57 us
where the time goes in v2:
time: 14.6 us; the launch traced here: 14.5 us
  Pallas kernels  12.9 us (88%)
  local copies, waits for them, and re-layouts  1.57 us (11%)
    pallas_call x1, Pallas kernels, body(): pl.pallas_call(functools.partial(kernel, n, nt), out_shape=jax.ShapeDtype...  12.9 us
    unnamed x1, local copies, waits for them, and re-layouts  1.57 us

profile of v2, /device:TPU:0, one launch (start us, length us, event | category | flops | bytes accessed | tf_op | source)
XLA Modules:
  0.0 14.5 jit_solution(6215376188451260623)
XLA Ops:
  0.0 12.9 %shard_map.37 = f32[16,8,256]{2,1,0:T(8,128)} custom-call(f32[16,8,256]{2,1,0:T(8,128)} %c_hbm.1, s32[16,8,256]{2,1,0:T(8,128)} %m_hbm.1, f32[16,8,256]{2,1,0:T(8,128)} %v_hbm.1), custom_call_target="tpu_custom_call" | custom-call | tf_op jit(solution)/shard_map/pallas_call | solution.py:300
  12.9 1.6 %copy.5 = f32[16,8,256]{2,1,0:T(8,128)} copy(f32[16,8,256]{2,1,0:T(8,128)} %shard_map.37) | data formatting | bytes 262144

commit v3 on v2

--- a/solution.py
+++ b/solution.py
@@ -13,19 +13,16 @@
 
 
 def kernel(
-    n, nt, c_hbm, m_hbm, v_hbm, out, c_s, m_s, v_s, ts, tr, axs, axr, rhs_s, cond, pair, chip, xx, xs, xr,
-    load_sem, t_send, t_recv, a_send, a_recv, p_send, p_recv, g_send, g_recv, x_send, x_recv,
+    n, nt, c_hbm, m_hbm, v_hbm, out, c_s, m_s, v_s, ts, tr, axs, axr, rhs_s, cond_c, cond_r, segs_c, segs_r, xx, xs, xr,
+    load_sem, t_send, t_recv, a_send, a_recv, g_send, g_recv, x_send, x_recv, up_sem,
 ):
     cells, rows, width = c_s.shape
     half = width // 2
-    chips = n // 2
     me = lax.axis_index("axial")
     mt = lax.axis_index("trans")
     last = cells - 1
-    q, core = me // 2, lax.rem(me, 2)
+    core = lax.rem(me, 2)
     sibling = me + 1 - 2 * core
-    beyond = me - 1 + 2 * core
-    has_beyond = jnp.logical_and(beyond >= 0, beyond < n)
 
     loads = [
         pltpu.make_async_copy(src, dst, load_sem.at[k])
@@ -38,24 +35,14 @@
     has_before, has_after = mt > 0, mt < nt - 1
     has_prev, has_next = me > 0, me < n - 1
 
-    @pl.when(has_before)
-    def _():
-        pl.semaphore_signal(barrier, inc=1, device_id=(me, mt - 1), device_id_type=MESH)
-
     @pl.when(has_after)
     def _():
         pl.semaphore_signal(barrier, inc=1, device_id=(me, mt + 1), device_id_type=MESH)
 
-    for d in range(chips - 1, 0, -1):
+    for d in range(n - 1, 0, -1):
         pl.semaphore_signal(
-            barrier, inc=1, device_id=(2 * lax.bitwise_xor(q, d) + core, mt), device_id_type=MESH
+            barrier, inc=1, device_id=(lax.bitwise_xor(me, d), mt), device_id_type=MESH
         )
-
-    @pl.when(has_beyond)
-    def _():
-        pl.semaphore_signal(barrier, inc=1, device_id=(beyond, mt), device_id_type=MESH)
-
-    pl.semaphore_signal(barrier, inc=1, device_id=(sibling, mt), device_id_type=MESH)
 
     @pl.when(jnp.logical_not(has_before))
     def _():
@@ -87,8 +74,7 @@
         axs[e, 1] = ph[i]
         axs[e, 2] = v[i]
 
-    here = [flag.astype(jnp.int32) for flag in (has_before, has_after, has_beyond)]
-    pl.semaphore_wait(barrier, chips + sum(here))
+    pl.semaphore_wait(barrier, n - 1 + has_before.astype(jnp.int32))
 
     def t_copy(e):
         return pltpu.make_async_remote_copy(
@@ -103,8 +89,12 @@
         )
 
     sides = ((0, has_before, has_prev), (1, has_after, has_next))
-    for e, has_t, _ in sides:
-        pl.when(has_t)(lambda e=e: t_copy(e).start())
+
+    @pl.when(has_before)
+    def _():
+        pl.semaphore_signal(up_sem, inc=1, device_id=(me, mt - 1), device_id_type=MESH)
+        t_copy(0).start()
+
     for e, _, has_a in sides:
         pl.when(has_a)(lambda e=e: a_copy(e).start())
 
@@ -145,6 +135,11 @@
         eps = lo(i) * qinv[i]
         reach = beta[i] if i == last - 1 else beta[i] * reach
 
+    @pl.when(has_after)
+    def _():
+        pl.semaphore_wait(up_sem, 1)
+        t_copy(1).start()
+
     for e, _, has_a in sides:
         pl.when(has_a)(lambda e=e: a_copy(1 - e).wait_recv())
 
@@ -163,14 +158,30 @@
     give = keep * spr_0
     far = spike[last - 1]
 
-    def put(k, value):
-        cond[0, k] = value[:, :half]
-        cond[1, k] = value[:, half:]
-
-    put(0, -lo(last) * far * a0)
-    put(1, 1.0 + spr[-1] + low_n - lo(last) * (far * b0 + gamma[last - 1]))
-    put(2, -give * a0)
-    put(3, -give * b0)
+    conds, segs = (cond_c, cond_r), (segs_c, segs_r)
+
+    def put(part, k, value):
+        conds[part][0, k] = value[:, :half]
+        conds[part][1, k] = value[:, half:]
+
+    def g_copy(part, d):
+        to = lax.bitwise_xor(me, d)
+        return pltpu.make_async_remote_copy(
+            src_ref=conds[part].at[lax.rem(to, 2)], dst_ref=segs[part].at[me],
+            send_sem=g_send.at[part, d], recv_sem=g_recv.at[part, d], device_id=(to, mt),
+            device_id_type=MESH,
+        )
+
+    def send_rows(part):
+        for d in range(n - 1, 0, -1):
+            g_copy(part, d).start()
+        segs[part][me] = conds[part][core]
+
+    put(0, 0, -lo(last) * far * a0)
+    put(0, 1, 1.0 + spr[-1] + low_n - lo(last) * (far * b0 + gamma[last - 1]))
+    put(0, 2, -give * a0)
+    put(0, 3, -give * b0)
+    send_rows(0)
 
     for e, has_t, _ in sides:
         pl.when(has_t)(lambda e=e: t_copy(1 - e).wait_recv())
@@ -186,36 +197,10 @@
     for i in range(last - 1, 0, -1):
         back = r[i] * qinv[i] if i == last - 1 else r[i] * qinv[i] + beta[i] * back
     c0 = w * (r[0] + flux_0 + up(0) * back)
-    put(4, r[last] - flux_n + lo(last) * (far * c0 + partial[last - 1]))
-    put(5, give * c0)
-
-    p_copy = pltpu.make_async_remote_copy(
-        src_ref=cond.at[1 - core], dst_ref=pair, send_sem=p_send.at[0], recv_sem=p_recv.at[0],
-        device_id=(sibling, mt), device_id_type=MESH,
-    )
-    p_copy.start()
-
-    def g_copy(d):
-        return pltpu.make_async_remote_copy(
-            src_ref=chip.at[q], dst_ref=chip.at[q], send_sem=g_send.at[d], recv_sem=g_recv.at[d],
-            device_id=(2 * lax.bitwise_xor(q, d) + core, mt), device_id_type=MESH,
-        )
-
-    own = cond[core]
-    first = core == 0
-    p_copy.wait_recv()
-    other = pair[...]
-    l_a, d_a, u1_a, u2_a, f_a, u3_a = [jnp.where(first, own[k], other[k]) for k in range(6)]
-    l_b, d_b, u1_b, u2_b, f_b, u3_b = [jnp.where(first, other[k], own[k]) for k in range(6)]
-    inv = 1.0 / (d_a + u1_b)
-    la, ua, fa = inv * l_a, inv * u2_b, inv * (f_a + u3_b)
-    merged = (
-        -l_b * la, d_b - l_b * ua, u1_a - u2_a * la, -u2_a * ua, f_b - l_b * fa, u3_a - u2_a * fa
-    )
-    for k, value in enumerate(merged):
-        chip[q, k] = value
-    for d in range(chips - 1, 0, -1):
-        g_copy(d).start()
+    put(1, 0, r[last] - flux_n + lo(last) * (far * c0 + partial[last - 1]))
+    put(1, 1, give * c0)
+
+    send_rows(1)
 
     from_first, from_last, fixed = {}, {}, {}
     for i in range(last - 1, 0, -1):
@@ -226,50 +211,54 @@
             from_last[i] = gamma[i] * from_last[i + 1]
             fixed[i] = partial[i] + gamma[i] * fixed[i + 1]
 
-    for d in range(1, chips):
-        g_copy(d).wait_recv()
-    side, free = {}, {}
-
-    def row(j):
-        above = j + 1 < chips
-        diag = chip[j, 1] + chip[j + 1, 2] if above else chip[j, 1]
-        right = chip[j, 4] + chip[j + 1, 5] if above else chip[j, 4]
-        return chip[j, 0], diag, chip[j + 1, 3] if above else None, right
-
-    middle = chips // 2
-    for j in range(middle):
-        lower, diag, upper, right = row(j)
-        if j > 0:
-            diag, right = diag - lower * side[j - 1], right - lower * free[j - 1]
-        inv = 1.0 / diag
-        side[j], free[j] = inv * upper, inv * right
-    for j in range(chips - 1, middle - 1, -1):
-        lower, diag, upper, right = row(j)
-        if j + 1 < chips:
-            diag, right = diag - upper * side[j + 1], right - upper * free[j + 1]
-        inv = 1.0 / diag
-        side[j], free[j] = inv * lower, inv * right
-    x = (free[middle] - side[middle] * free[middle - 1]) / (1.0 - side[middle] * side[middle - 1])
+    for d in range(1, n):
+        g_copy(0, d).wait_recv()
+    middle = n // 2
+    side, scale, inward = {}, {}, {}
+    for j in [*range(middle), *range(n - 1, middle - 1, -1)]:
+        above = j + 1 < n
+        lower, diag = segs_c[j, 0], segs_c[j, 1]
+        upper = None
+        if above:
+            diag, upper = diag + segs_c[j + 1, 2], segs_c[j + 1, 3]
+        if j < middle:
+            inward[j], outward, before = lower, upper, j - 1
+        else:
+            inward[j], outward, before = upper, lower, j + 1
+        if before in side:
+            diag = diag - inward[j] * side[before]
+        scale[j] = 1.0 / diag
+        side[j] = scale[j] * outward
+    meet = 1.0 / (1.0 - side[middle] * side[middle - 1])
+
+    for d in range(1, n):
+        g_copy(1, d).wait_recv()
+    free = {}
+    for j in [*range(middle), *range(n - 1, middle - 1, -1)]:
+        right = segs_r[j, 0] + segs_r[j + 1, 1] if j + 1 < n else segs_r[j, 0]
+        before = j - 1 if j < middle else j + 1
+        if before in free:
+            right = right - inward[j] * free[before]
+        free[j] = scale[j] * right
+    x = meet * (free[middle] - side[middle] * free[middle - 1])
     xx[0] = jnp.zeros_like(x)
     xx[middle + 1] = x
     down = up_x = x
     for j in range(middle - 1, -1, -1):
         down = free[j] - side[j] * down
         xx[j + 1] = down
-    for j in range(middle + 1, chips):
+    for j in range(middle + 1, n):
         up_x = free[j] - side[j] * up_x
         xx[j + 1] = up_x
-    x_p, x_b = xx[q], xx[q + 1]
-    x_a = fa - la * x_p - ua * x_b
-    xs[0] = jnp.where(first, x_a, x_p)
-    xs[1] = jnp.where(first, x_b, x_a)
+    xs[0] = xx[sibling]
+    xs[1] = xx[sibling + 1]
     x_copy = pltpu.make_async_remote_copy(
         src_ref=xs, dst_ref=xr.at[core], send_sem=x_send.at[0], recv_sem=x_recv.at[0],
         device_id=(sibling, mt), device_id_type=MESH,
     )
     x_copy.start()
-    xr[core, 0] = jnp.where(first, x_p, x_a)
-    xr[core, 1] = jnp.where(first, x_a, x_b)
+    xr[core, 0] = xx[me]
+    xr[core, 1] = xx[me + 1]
     pltpu.make_async_remote_copy(
         src_ref=xs, dst_ref=xr.at[1 - core], send_sem=x_send.at[0], recv_sem=x_recv.at[0],
         device_id=(sibling, mt), device_id_type=MESH,
@@ -285,9 +274,9 @@
     for e, has_t, has_a in sides:
         pl.when(has_t)(lambda e=e: t_copy(e).wait_send())
         pl.when(has_a)(lambda e=e: a_copy(e).wait_send())
-    p_copy.wait_send()
-    for d in range(1, chips):
-        g_copy(d).wait_send()
+    for d in range(1, n):
+        g_copy(0, d).wait_send()
+        g_copy(1, d).wait_send()
     x_copy.wait_send()
 
 
@@ -311,14 +300,16 @@
             pltpu.VMEM((2, 3, rows, width), f32),
             pltpu.VMEM((2, 3, rows, width), f32),
             pltpu.VMEM((cells, rows, width), f32),
-            pltpu.VMEM((2, 6, rows, width // 2), f32),
-            pltpu.VMEM((6, rows, width // 2), f32),
-            pltpu.VMEM((n // 2, 6, rows, width // 2), f32),
-            pltpu.VMEM((n // 2 + 1, rows, width // 2), f32),
+            pltpu.VMEM((2, 4, rows, width // 2), f32),
+            pltpu.VMEM((2, 2, rows, width // 2), f32),
+            pltpu.VMEM((n, 4, rows, width // 2), f32),
+            pltpu.VMEM((n, 2, rows, width // 2), f32),
+            pltpu.VMEM((n + 1, rows, width // 2), f32),
             pltpu.VMEM((2, rows, width // 2), f32),
             pltpu.VMEM((2, 2, rows, width // 2), f32),
             dma((3,)), dma((2,)), dma((2,)), dma((2,)), dma((2,)),
-            dma((1,)), dma((1,)), dma((n // 2,)), dma((n // 2,)), dma((1,)), dma((1,)),
+            dma((2, n)), dma((2, n)), dma((1,)), dma((1,)),
+            pltpu.SemaphoreType.REGULAR,
         ],
         compiler_params=pltpu.CompilerParams(
             collective_id=0, has_side_effects=True

time: 14.6 us -> 14.3 us (0.979)
  Pallas kernels: 12.9 us -> 12.6 us
    pallas_call x1, Pallas kernels: 12.9 us -> 12.6 us  [body(): pl.pallas_call(functools.partial(kernel, n, nt), out_shape=jax.ShapeDtype...]
where the time goes in v3:
time: 14.3 us; the launch traced here: 14.2 us
  Pallas kernels  12.6 us (88%)
  local copies, waits for them, and re-layouts  1.57 us (11%)
    pallas_call x1, Pallas kernels, body(): pl.pallas_call(functools.partial(kernel, n, nt), out_shape=jax.ShapeDtype...  12.6 us
    unnamed x1, local copies, waits for them, and re-layouts  1.57 us

profile of v3, /device:TPU:0, one launch (start us, length us, event | category | flops | bytes accessed | tf_op | source)
XLA Modules:
  0.0 14.2 jit_solution(9371858610355107718)
XLA Ops:
  0.0 12.6 %shard_map.37 = f32[16,8,256]{2,1,0:T(8,128)} custom-call(f32[16,8,256]{2,1,0:T(8,128)} %c_hbm.1, s32[16,8,256]{2,1,0:T(8,128)} %m_hbm.1, f32[16,8,256]{2,1,0:T(8,128)} %v_hbm.1), custom_call_target="tpu_custom_call" | custom-call | tf_op jit(solution)/shard_map/pallas_call | solution.py:289
  12.6 1.6 %copy.5 = f32[16,8,256]{2,1,0:T(8,128)} copy(f32[16,8,256]{2,1,0:T(8,128)} %shard_map.37) | data formatting | bytes 262144

commit v4 on v3

--- a/solution.py
+++ b/solution.py
@@ -90,18 +90,24 @@
 
     sides = ((0, has_before, has_prev), (1, has_after, has_next))
 
+    for e, _, has_a in sides:
+        pl.when(has_a)(lambda e=e: a_copy(e).start())
+
     @pl.when(has_before)
     def _():
         pl.semaphore_signal(up_sem, inc=1, device_id=(me, mt - 1), device_id_type=MESH)
         t_copy(0).start()
 
-    for e, _, has_a in sides:
-        pl.when(has_a)(lambda e=e: a_copy(e).start())
 
     share = 0.5 * (ph[:-1] + ph[1:])
     spr = axial_number * share
     low = 0.5 * (v[:-1] + v[1:]) * share + spr
     flux = low * c[:-1] - spr * c[1:]
+    @pl.when(has_after)
+    def _():
+        pl.semaphore_wait(up_sem, 1)
+        t_copy(1).start()
+
     lane = lax.broadcasted_iota(jnp.int32, c.shape, 2)
     ph_l = jnp.where(lane == 0, 0.0, pltpu.roll(ph, 1, 2))
     c_l = jnp.where(lane == 0, 0.0, pltpu.roll(c, 1, 2))
@@ -134,11 +140,6 @@
         beta[i] = up(i) * qinv[i]
         eps = lo(i) * qinv[i]
         reach = beta[i] if i == last - 1 else beta[i] * reach
-
-    @pl.when(has_after)
-    def _():
-        pl.semaphore_wait(up_sem, 1)
-        t_copy(1).start()
 
     for e, _, has_a in sides:
         pl.when(has_a)(lambda e=e: a_copy(1 - e).wait_recv())

time: 14.3 us -> 14.2 us (level)
    pallas_call x1, Pallas kernels: 12.6 us -> 12.5 us  [body(): pl.pallas_call(functools.partial(kernel, n, nt), out_shape=jax.ShapeDtype...]
where the time goes in v4:
time: 14.2 us; the launch traced here: 14 us
  Pallas kernels  12.5 us (88%)
  local copies, waits for them, and re-layouts  1.57 us (11%)
    pallas_call x1, Pallas kernels, body(): pl.pallas_call(functools.partial(kernel, n, nt), out_shape=jax.ShapeDtype...  12.5 us
    unnamed x1, local copies, waits for them, and re-layouts  1.57 us

profile of v4, /device:TPU:0, one launch (start us, length us, event | category | flops | bytes accessed | tf_op | source)
XLA Modules:
  0.0 14.0 jit_solution(14853677345147527748)
XLA Ops:
  0.0 12.5 %shard_map.37 = f32[16,8,256]{2,1,0:T(8,128)} custom-call(f32[16,8,256]{2,1,0:T(8,128)} %c_hbm.1, s32[16,8,256]{2,1,0:T(8,128)} %m_hbm.1, f32[16,8,256]{2,1,0:T(8,128)} %v_hbm.1), custom_call_target="tpu_custom_call" | custom-call | tf_op jit(solution)/shard_map/pallas_call | solution.py:290
  12.5 1.6 %copy.5 = f32[16,8,256]{2,1,0:T(8,128)} copy(f32[16,8,256]{2,1,0:T(8,128)} %shard_map.37) | data formatting | bytes 262144
